TPU v7x, 32 devices: a whole 2x2x4 slice. The times are simulated.
32 devices in a mesh: groups: 2 (over x), seq: 16 (over z, y, core).
Axes of the slice: x: 2, y: 2, z: 4, core: 2. Of those that a mesh axis runs over, the one named last changes fastest.
Arguments:
- activations: bfloat16 [4096, 8192], P(('groups', 'seq')), parts along dimension 0, may hold values from -6 to 6
- out_grads: bfloat16 [4096, 14336], P(('groups', 'seq')), parts along dimension 0, may hold values from -6 to 6
- query_grad: bfloat16 [2, 16384, 14336], P(None, ('groups', 'seq')), parts along dimension 1, may hold values from -0.00015258789 to 0.00015258789
- segment_ids: int32 [32, 128], P(('groups', 'seq')), parts along dimension 0, may hold values from 0 to 3, never falling along the last dimension, each value on 1 to 64 neighbouring positions
- sequence_ids: int32 [32, 4], P(('groups', 'seq')), parts along dimension 0, may hold values from 0 to 31
Outputs:
- scores: float32 [2, 64], P(None, ('groups', 'seq')), parts along dimension 1
There are 2 independent parts, one for each index of `groups`. A program takes and returns all parts, laid end to end along the dimension named above; each array names one. Nothing has to cross between parts.
All inputs are finite; a program needn't handle non-finite values.
Results may differ from a plain program's by a relative error of at most 0.0003.
Values may be sent and summed in bfloat16 or wider, within the bound.
A program may use at most 192 MiB of HBM per device.

v0:
```python
import jax
import jax.numpy as jnp
from jax import lax
from jax.sharding import PartitionSpec as P

SEGS = 4
SEQS_DEV = 2


def shifted(x, axis, by):
    peers = lax.axis_size(axis)
    return lax.ppermute(x, axis, [(i, (i + by) % peers) for i in range(peers)])


def membership(segments, seqids, total):
    seg_hot = (segments[0][:, None] == jnp.arange(SEGS, dtype=jnp.int32)[None, :]).astype(
        jnp.float32
    )
    seq_hot = (seqids[0][:, None] == jnp.arange(total, dtype=jnp.int32)[None, :]).astype(
        jnp.float32
    )
    return jnp.dot(seg_hot, seq_hot, precision=lax.Precision.HIGHEST)


def band_term(columns, grads, bands):
    grads32 = grads.astype(jnp.float32)
    results = []
    for query in range(bands.shape[0]):
        h = jnp.dot(columns, bands[query], preferred_element_type=jnp.float32)
        results.append(jnp.sum(h * grads32, axis=1))
    return jnp.stack(results)


def local(activations, out_grads, query_grad, segment_ids, sequence_ids):
    count = lax.axis_size("seq")
    here = lax.axis_index("seq")
    band_rows = query_grad.shape[1]
    width = out_grads.shape[1]
    total = SEQS_DEV * count
    member = membership(segment_ids, sequence_ids, total)

    def columns_of(step):
        start = (here - step) % count * band_rows
        return lax.dynamic_slice_in_dim(activations, start, band_rows, 1)

    partial_value = band_term(columns_of(0), out_grads, query_grad)
    member_wire = member.astype(jnp.bfloat16)
    near_pack = jnp.concatenate([columns_of(1), out_grads, member_wire], axis=1)
    far_pack = jnp.concatenate([columns_of(2), out_grads, member_wire], axis=1)
    near_got = shifted(near_pack, "seq", -1)
    far_got = shifted(far_pack, "seq", -2)
    terms = jnp.dot(partial_value, member, precision=lax.Precision.HIGHEST)
    for got in (near_got, far_got):
        got_cols = got[:, :band_rows]
        got_grads = got[:, band_rows : band_rows + width]
        got_member = got[:, band_rows + width :].astype(jnp.float32)
        got_partial = band_term(got_cols, got_grads, query_grad)
        terms = terms + jnp.dot(got_partial, got_member, precision=lax.Precision.HIGHEST)
    summed = lax.psum(terms, "seq")
    mine = lax.dynamic_slice_in_dim(summed, here * SEQS_DEV, SEQS_DEV, 1)
    return mine


def solution(mesh):
    placed = (
        P(("groups", "seq"), None),
        P(("groups", "seq"), None),
        P(None, ("groups", "seq"), None),
        P(("groups", "seq"), None),
        P(("groups", "seq"), None),
    )
    return jax.shard_map(
        local, mesh=mesh, in_specs=placed, out_specs=P(None, ("groups", "seq")), check_vma=False
    )
```

profile of v0, /device:TPU:0, one launch (start us, length us, event | category | flops | bytes accessed | tf_op | source)
XLA Modules:
  0.0 224.2 jit_solution(14493295139500616821)
XLA Ops:
  0.0 0.0 copy-start.3
  0.0 0.0 copy-start.4
  0.0 1.0 constant_dynamic-slice_fusion.1
  1.0 0.1 copy.16
  1.1 6.1 %copy.9 = bf16[128,14336]{0,1:T(8,128)(2,1)} copy(bf16[128,14336]{1,0:T(8,128)(2,1)} %param.6) | data formatting | bytes 7340032 | tf_op args[1]
  7.2 0.1 copy.14
  7.3 0.0 copy-done.3
  7.3 0.0 copy-done.4
  7.3 0.2 fusion.56
  7.6 10.7 %pad_maximum_fusion = (bf16[128,14880]{0,1:T(8,128)(2,1)}, bf16[128,14880]{0,1:T(8,128)(2,1)}) fusion(bf16[128,32]{0,1:T(8,128)(2,1)S(1)} %get-tuple-element.9, bf16[128,512]{0,1:T(8,128)(2,1)S(1)} %copy.16, bf16[128,14336]{0,1:T(8,128)(2,1)} %copy.9, bf16[128,512]{0,1:T(8,128)(2,1)S(1)} %copy.14), kind=kLoop, calls=%fused_computation.18 | loop fusion | flops 19046400 | bytes 11558912 | tf_op jit(solution)/shard_map/concatenate | solution.py:49
  18.3 5.4 %collective-permute-start = (bf16[128,14880]{0,1:T(8,128)(2,1)}, bf16[128,14880]{0,1:T(8,128)(2,1)}, u32[]{:S(2)}, u32[]{:S(2)}) collective-permute-start(bf16[128,14880]{0,1:T(8,128)(2,1)} %get-tuple-element.6), channel_id=1, source_target_pairs={{0,15},{1,0},{2,1},{3,2},{4,3},{5,4},{6,5},{7,6},{8,7},{9,8},{10,9... | collective-permute-start | bytes 11427848 | tf_op jit(solution)/shard_map/ppermute | solution.py:12
  23.8 0.6 collective-permute-start.1
  24.3 0.0 copy-start
  24.3 8.6 %fusion.15 = f32[128]{0:T(128)S(1)} fusion(bf16[128,14336]{1,0:T(8,128)(2,1)} %param.6, bf16[2,512,14336]{2,1,0:T(8,128)(2,1)} %param.7, bf16[128,8192]{1,0:T(8,128)(2,1)} %param.5, s32[]{:T(128)S(6)} %select_n.28), kind=kOutput, calls=%fused_computation.21 | convolution fusion | flops 1884553088 | bytes 18481668 | tf_op jit(solution)/shard_map/dot_general | solution.py:29
  32.9 0.0 copy-done
  32.9 7.7 %fusion.12 = f32[128]{0:T(128)S(1)} fusion(bf16[128,14336]{1,0:T(8,128)(2,1)S(1)} %copy-done, bf16[2,512,14336]{2,1,0:T(8,128)(2,1)} %param.7, bf16[128,8192]{1,0:T(8,128)(2,1)} %param.5, s32[]{:T(128)S(6)} %select_n.28), kind=kOutput, calls=%fused_computation.20 | convolution fusion | flops 1884553088 | bytes 18481668 | tf_op jit(solution)/shard_map/dot_general | solution.py:29
  40.6 0.1 fusion.40
  40.8 65.9 %collective-permute-done = bf16[128,14880]{0,1:T(8,128)(2,1)} collective-permute-done((bf16[128,14880]{0,1:T(8,128)(2,1)}, bf16[128,14880]{0,1:T(8,128)(2,1)}, u32[]{:S(2)}, u32[]{:S(2)}) %collective-permute-start) | collective-permute-done | bytes 3809312 | tf_op jit(solution)/shard_map/ppermute | solution.py:12
  106.7 3.4 %slice.37 = bf16[128,14336]{0,1:T(8,128)(2,1)} slice(bf16[128,14880]{0,1:T(8,128)(2,1)} %collective-permute-done), slice={[0:128], [512:14848]} | slice | bytes 7340032 | tf_op jit(solution)/shard_map/slice | solution.py:55
  110.1 6.1 %copy.15 = bf16[128,14336]{1,0:T(8,128)(2,1)} copy(bf16[128,14336]{0,1:T(8,128)(2,1)} %slice.37) | data formatting | bytes 7340032
  116.2 31.4 %collective-permute-done.1 = bf16[128,14880]{0,1:T(8,128)(2,1)} collective-permute-done((bf16[128,14880]{0,1:T(8,128)(2,1)}, bf16[128,14880]{0,1:T(8,128)(2,1)}, u32[]{:S(2)}, u32[]{:S(2)}) %collective-permute-start.1) | collective-permute-done | bytes 3809312 | tf_op jit(solution)/shard_map/ppermute | solution.py:12
  147.6 3.4 %slice.40 = bf16[128,14336]{0,1:T(8,128)(2,1)} slice(bf16[128,14880]{0,1:T(8,128)(2,1)} %collective-permute-done.1), slice={[0:128], [512:14848]} | slice | bytes 7340032 | tf_op jit(solution)/shard_map/slice | solution.py:55
  151.1 6.0 %copy.17 = bf16[128,14336]{1,0:T(8,128)(2,1)} copy(bf16[128,14336]{0,1:T(8,128)(2,1)} %slice.40) | data formatting | bytes 7340032
  157.1 0.0 copy-start.1
  157.1 9.3 %fusion.21 = f32[128]{0:T(128)S(1)} fusion(bf16[128,14336]{1,0:T(8,128)(2,1)} %copy.15, bf16[2,512,14336]{2,1,0:T(8,128)(2,1)} %param.7, bf16[128,14880]{0,1:T(8,128)(2,1)} %collective-permute-done), kind=kOutput, calls=%fused_computation.23 | convolution fusion | flops 1884553088 | bytes 18481664 | tf_op jit(solution)/shard_map/dot_general | solution.py:29
  166.4 0.0 copy-done.1
  166.4 0.0 copy-start.2
  166.4 8.6 %fusion.18 = f32[128]{0:T(128)S(1)} fusion(bf16[128,14336]{1,0:T(8,128)(2,1)S(1)} %copy-done.1, bf16[2,512,14336]{2,1,0:T(8,128)(2,1)} %param.7, bf16[128,14880]{0,1:T(8,128)(2,1)} %collective-permute-done), kind=kOutput, calls=%fused_computation.22 | convolution fusion | flops 1884553088 | bytes 18481664 | tf_op jit(solution)/shard_map/dot_general | solution.py:29
  175.1 0.0 copy-done.2
  175.1 8.5 %fusion.27 = f32[128]{0:T(128)S(1)} fusion(bf16[128,14336]{1,0:T(8,128)(2,1)S(1)} %copy-done.2, bf16[2,512,14336]{2,1,0:T(8,128)(2,1)} %param.7, bf16[128,14880]{0,1:T(8,128)(2,1)} %collective-permute-done.1), kind=kOutput, calls=%fused_computation.25 | convolution fusion | flops 1884553088 | bytes 18481664 | tf_op jit(solution)/shard_map/dot_general | solution.py:29
  183.6 8.5 %fusion.24 = f32[128]{0:T(128)S(1)} fusion(bf16[128,14336]{1,0:T(8,128)(2,1)S(1)} %copy-done.2, bf16[2,512,14336]{2,1,0:T(8,128)(2,1)} %param.7, bf16[128,14880]{0,1:T(8,128)(2,1)} %collective-permute-done.1), kind=kOutput, calls=%fused_computation.24 | convolution fusion | flops 1884553088 | bytes 18481664 | tf_op jit(solution)/shard_map/dot_general | solution.py:29
  192.1 0.8 convolution_add_fusion.1
  192.9 0.8 convolution_add_fusion
  193.7 29.9 %psum.7 = f32[2,32]{1,0:T(2,128)S(1)} all-reduce(f32[2,32]{1,0:T(2,128)S(1)} %convolution_add_fusion), channel_id=1, replica_groups=mesh['groups'=2,'seq'=16] {'seq'}, use_global_device_ids=true, to_apply=%region_6.7 | all-reduce | flops 64 | bytes 512 | tf_op jit(solution)/shard_map/psum | solution.py:59
  223.6 0.6 constant_dynamic-slice_fusion
Async XLA Ops:
  0.0 7.3 %copy-start.3 = (s32[1,4]{1,0:T(1,128)S(1)}, s32[1,4]{1,0:T(1,128)}, u32[]{:S(2)}) copy-start(s32[1,4]{1,0:T(1,128)} %param.9) | copy-start | bytes 52
  0.0 7.3 %copy-start.4 = (s32[1,128]{1,0:T(1,128)S(1)}, s32[1,128]{1,0:T(1,128)}, u32[]{:S(2)}) copy-start(s32[1,128]{1,0:T(1,128)} %param.8) | copy-start | bytes 1540
  18.3 88.4 %collective-permute-start = (bf16[128,14880]{0,1:T(8,128)(2,1)}, bf16[128,14880]{0,1:T(8,128)(2,1)}, u32[]{:S(2)}, u32[]{:S(2)}) collective-permute-start(bf16[128,14880]{0,1:T(8,128)(2,1)} %get-tuple-element.6), channel_id=1, source_target_pairs={{0,15},{1,0},{2,1},{3,2},{4,3},{5,4},{6,5},{7,6},{8,7},{9,8},{10,9... | collective-permute-start | bytes 11427848 | tf_op jit(solution)/shard_map/ppermute | solution.py:12
  23.8 123.8 %collective-permute-start.1 = (bf16[128,14880]{0,1:T(8,128)(2,1)}, bf16[128,14880]{0,1:T(8,128)(2,1)}, u32[]{:S(2)}, u32[]{:S(2)}) collective-permute-start(bf16[128,14880]{0,1:T(8,128)(2,1)} %get-tuple-element.5), channel_id=1, source_target_pairs={{0,14},{1,15},{2,0},{3,1},{4,2},{5,3},{6,4},{7,5},{8,6},{9,7},{10,... | collective-permute-start | bytes 11427848 | tf_op jit(solution)/shard_map/ppermute | solution.py:12
  24.3 8.6 %copy-start = (bf16[128,14336]{1,0:T(8,128)(2,1)S(1)}, bf16[128,14336]{1,0:T(8,128)(2,1)}, u32[]{:S(2)}) copy-start(bf16[128,14336]{1,0:T(8,128)(2,1)} %param.6) | copy-start | bytes 11010052
  157.1 9.3 %copy-start.1 = (bf16[128,14336]{1,0:T(8,128)(2,1)S(1)}, bf16[128,14336]{1,0:T(8,128)(2,1)}, u32[]{:S(2)}) copy-start(bf16[128,14336]{1,0:T(8,128)(2,1)} %copy.15) | copy-start | bytes 11010052
  166.4 8.6 %copy-start.2 = (bf16[128,14336]{1,0:T(8,128)(2,1)S(1)}, bf16[128,14336]{1,0:T(8,128)(2,1)}, u32[]{:S(2)}) copy-start(bf16[128,14336]{1,0:T(8,128)(2,1)} %copy.17) | copy-start | bytes 11010052
where the time goes:
time: 225 us; the launch traced here: 224 us
  waiting for transfers between devices  97.3 us (43%)
  matrix products  53.3 us (24%)
  blocking collectives  29.9 us (13%)
  local copies, waits for them, and re-layouts  27 us (12%)
  other arithmetic  10.7 us (5%)
  starting transfers between devices  6.01 us (3%)
    ppermute x2, waiting for transfers between devices, shifted(): return lax.ppermute(x, axis, [(i, (i + by) % peers) for i in range(peers)])  97.3 us
    dot_general x6, matrix products, band_term(): h = jnp.dot(columns, bands[query], preferred_element_type=jnp.float32)  51.2 us
    psum x1, blocking collectives, local(): summed = lax.psum(terms, 'seq')  29.9 us
    unnamed x15, local copies, waits for them, and re-layouts  18.4 us
    concatenate x1, other arithmetic, local(): far_pack = jnp.concatenate([columns_of(2), out_grads, member_wire], axis=1)  10.7 us
    slice x2, local copies, waits for them, and re-layouts, local(): got_grads = got[:, band_rows:band_rows + width]  6.86 us
    ppermute x2, starting transfers between devices, shifted(): return lax.ppermute(x, axis, [(i, (i + by) % peers) for i in range(peers)])  6.01 us
  transfers between devices with their start and end apart: 2, of which 2 were waited for; matrix products, arithmetic and copies ran while one was open for 12% of the time, Pallas kernels for 0%

commit v1 on v0

v1 whole, which is shorter than its diff:
```python
import functools
import math

import jax
import jax.numpy as jnp
from jax import lax
from jax.experimental import pallas as pl
from jax.experimental.pallas import tpu as pltpu
from jax.sharding import PartitionSpec as P

SEGS = 4
SEQS_DEV = 2
MESH = pl.DeviceIdType.MESH


def kernel(
    count,
    chunk,
    act_ref,
    grad_ref,
    query_ref,
    seg_ref,
    seq_ref,
    out_ref,
    held_query,
    held_grad,
    held_act,
    held_sid,
    acc,
    term_mine,
    term_got,
    query_sem,
    own_sem,
    act_sem,
    far_send,
    far_recv,
    near_send,
    near_recv,
    side_send,
    side_recv,
    term_send,
    term_recv,
):
    group = lax.axis_index("groups")
    me = lax.axis_index("seq")
    queries, band, width = query_ref.shape
    tokens = grad_ref.shape[0]
    chunks = width // chunk
    pad = term_mine.shape[1]
    even = lax.rem(me, 2) == 0
    back1 = lax.rem(me + count - 1, count)
    back2 = lax.rem(me + count - 2, count)
    ahead1 = lax.rem(me + 1, count)

    def columns(owner):
        return act_ref.at[:, pl.ds(pl.multiple_of(owner * band, band), band)]

    def span(k):
        return pl.ds(pl.multiple_of(k * chunk, chunk), chunk)

    def query_copy(k):
        return pltpu.make_async_copy(
            query_ref.at[:, :, span(k)], held_query.at[k], query_sem.at[k]
        )

    def own_copy(k):
        return pltpu.make_async_copy(grad_ref.at[:, span(k)], held_grad.at[0, k], own_sem.at[k])

    def far_copy(k):
        return pltpu.make_async_remote_copy(
            src_ref=grad_ref.at[:, span(k)],
            dst_ref=held_grad.at[2, k],
            send_sem=far_send.at[k],
            recv_sem=far_recv.at[k],
            device_id=(group, back2),
            device_id_type=MESH,
        )

    def near_copy(k):
        return pltpu.make_async_remote_copy(
            src_ref=grad_ref.at[:, span(k)],
            dst_ref=held_grad.at[1, k],
            send_sem=near_send.at[k],
            recv_sem=near_recv.at[k],
            device_id=(group, back1),
            device_id_type=MESH,
        )

    def relay_copy(k):
        return pltpu.make_async_remote_copy(
            src_ref=held_grad.at[2, k],
            dst_ref=held_grad.at[1, k],
            send_sem=near_send.at[k],
            recv_sem=near_recv.at[k],
            device_id=(group, ahead1),
            device_id_type=MESH,
        )

    def side_copies():
        made = []
        for slot, target in ((1, back1), (2, back2)):
            for kind, source, place in (
                (0, columns(target), held_act.at[slot]),
                (1, held_sid.at[0], held_sid.at[slot]),
            ):
                index = 2 * (slot - 1) + kind
                made.append(
                    pltpu.make_async_remote_copy(
                        src_ref=source,
                        dst_ref=place,
                        send_sem=side_send.at[index],
                        recv_sem=side_recv.at[index],
                        device_id=(group, target),
                        device_id_type=MESH,
                    )
                )
        return made

    def term_copy(d):
        return pltpu.make_async_remote_copy(
            src_ref=term_mine,
            dst_ref=term_got.at[d],
            send_sem=term_send.at[d],
            recv_sem=term_recv.at[d],
            device_id=(group, lax.rem(me + d, count)),
            device_id_type=MESH,
        )

    barrier = pltpu.get_barrier_semaphore()

    @pl.loop(1, count)
    def _(d):
        pl.semaphore_signal(
            barrier,
            inc=1,
            device_id=(group, lax.rem(me + d, count)),
            device_id_type=MESH,
        )

    sid = jnp.zeros((1, tokens), jnp.int32)
    for s in range(SEGS):
        sid = sid + jnp.where(seg_ref[...] == s, seq_ref[0, s], 0)
    held_sid[0] = jnp.broadcast_to(sid.astype(jnp.float32), held_sid.shape[1:])
    acc[...] = jnp.zeros_like(acc)
    pl.semaphore_wait(barrier, count - 1)

    @pl.loop(0, chunks)
    def _(k):
        far_copy(k).start()

    @pl.when(lax.rem(me, 2) == 1)
    def _():
        @pl.loop(0, chunks)
        def _(k):
            near_copy(k).start()

    for copy in side_copies():
        copy.start()
    own_act = pltpu.make_async_copy(columns(me), held_act.at[0], act_sem)
    own_act.start()

    @pl.loop(0, chunks)
    def _(k):
        query_copy(k).start()
        own_copy(k).start()

    def add(k, slot):
        for q in range(queries):
            acc[slot, q] += lax.dot_general(
                held_grad[slot, k],
                held_query[k, q],
                (((1,), (1,)), ((), ())),
                preferred_element_type=jnp.float32,
            )

    @pl.loop(0, chunks)
    def _(k):
        query_copy(k).wait()
        own_copy(k).wait()
        add(k, 0)
        far_copy(k).wait_recv()

        @pl.when(even)
        def _():
            relay_copy(k).start()

        add(k, 2)
        near_copy(k).wait_recv()
        add(k, 1)

    own_act.wait()
    for copy in side_copies():
        copy.wait_recv()
    lanes = lax.broadcasted_iota(jnp.int32, (tokens, pad), 1).astype(jnp.float32)
    rows = [jnp.zeros((1, pad), jnp.float32) for _ in range(queries)]
    for slot in range(3):
        ids = jnp.broadcast_to(held_sid[slot][0:1, :], (tokens, tokens)).T
        member = (lanes == ids[:, 0:1]).astype(jnp.float32)
        act = held_act[slot].astype(jnp.float32)
        for q in range(queries):
            value = jnp.sum(acc[slot, q] * act, axis=1, keepdims=True)
            rows[q] = rows[q] + jnp.sum(value * member, axis=0, keepdims=True)
    sub = lax.broadcasted_iota(jnp.int32, term_mine.shape, 0)
    mine = jnp.zeros(term_mine.shape, jnp.float32)
    for q in range(queries):
        mine = jnp.where(sub == q, jnp.broadcast_to(rows[q], term_mine.shape), mine)
    term_mine[...] = mine

    @pl.loop(1, count)
    def _(d):
        term_copy(d).start()

    @pl.loop(0, chunks)
    def _(k):
        far_copy(k).wait_send()
        near_copy(k).wait_send()

    for copy in side_copies():
        copy.wait_send()

    def gather(d, total):
        term_copy(d).wait_recv()
        return total + term_got[d]

    total = lax.fori_loop(1, count, gather, term_mine[...])
    lane = lax.broadcasted_iota(jnp.int32, total.shape, 1)
    spot = lax.broadcasted_iota(jnp.int32, out_ref.shape, 1)
    result = jnp.zeros(out_ref.shape, jnp.float32)
    for s in range(SEQS_DEV):
        picked = jnp.sum(
            jnp.where(lane == me * SEQS_DEV + s, total, 0.0), axis=1, keepdims=True
        )
        result = jnp.where(
            spot == s, jnp.broadcast_to(picked[:queries], out_ref.shape), result
        )
    out_ref[...] = result

    @pl.loop(1, count)
    def _(d):
        term_copy(d).wait_send()


def local(activations, out_grads, query_grad, segment_ids, sequence_ids):
    count = lax.axis_size("seq")
    queries, band, width = query_grad.shape
    tokens = out_grads.shape[0]
    chunk = math.gcd(width, 1024)
    chunks = width // chunk
    pad = -(-SEQS_DEV * count // 128) * 128
    sub = -(-queries // 8) * 8
    dma = pltpu.SemaphoreType.DMA
    whole = pl.BlockSpec(memory_space=pl.ANY)
    return pl.pallas_call(
        functools.partial(kernel, count, chunk),
        out_shape=jax.ShapeDtypeStruct((queries, SEQS_DEV), jnp.float32),
        in_specs=[
            whole,
            whole,
            whole,
            pl.BlockSpec(memory_space=pltpu.VMEM),
            pl.BlockSpec(memory_space=pltpu.SMEM),
        ],
        out_specs=pl.BlockSpec(memory_space=pltpu.VMEM),
        scratch_shapes=[
            pltpu.VMEM((chunks, queries, band, chunk), jnp.bfloat16),
            pltpu.VMEM((3, chunks, tokens, chunk), jnp.bfloat16),
            pltpu.VMEM((3, tokens, band), jnp.bfloat16),
            pltpu.VMEM((3, 8, tokens), jnp.float32),
            pltpu.VMEM((3, queries, tokens, band), jnp.float32),
            pltpu.VMEM((sub, pad), jnp.float32),
            pltpu.VMEM((count, sub, pad), jnp.float32),
            dma((chunks,)),
            dma((chunks,)),
            dma,
            dma((chunks,)),
            dma((chunks,)),
            dma((chunks,)),
            dma((chunks,)),
            dma((4,)),
            dma((4,)),
            dma((count,)),
            dma((count,)),
        ],
        compiler_params=pltpu.CompilerParams(
            collective_id=0, has_side_effects=True, vmem_limit_bytes=56 * 1024 * 1024
        ),
        cost_estimate=pl.CostEstimate(
            flops=6 * queries * tokens * band * width,
            bytes_accessed=2 * queries * band * width,
            transcendentals=0,
        ),
    )(activations, out_grads, query_grad, segment_ids, sequence_ids)


def solution(mesh):
    placed = (
        P(("groups", "seq"), None),
        P(("groups", "seq"), None),
        P(None, ("groups", "seq"), None),
        P(("groups", "seq"), None),
        P(("groups", "seq"), None),
    )
    return jax.shard_map(
        local, mesh=mesh, in_specs=placed, out_specs=P(None, ("groups", "seq")), check_vma=False
    )
```

time: 225 us -> 101 us (0.45)
  Pallas kernels: 0 us -> 99.8 us
  waiting for transfers between devices: 97.3 us -> 0 us
  matrix products: 53.3 us -> 0 us
  blocking collectives: 29.9 us -> 0 us
  local copies, waits for them, and re-layouts: 27 us -> 1.24 us
  other arithmetic: 10.7 us -> 0 us
  starting transfers between devices: 6.01 us -> 0 us
    pallas_call x0 -> x1, Pallas kernels: none -> 99.8 us  [local(): pl.pallas_call(functools.partial(kernel, count, chunk), out_shape=jax.Sha...]
    ppermute x2 -> x0, waiting for transfers between devices: 97.3 us -> none  [shifted(): return lax.ppermute(x, axis, [(i, (i + by) % peers) for i in range(peers)])]
    dot_general x10 -> x0, matrix products: 53.3 us -> none  [the longest x6 51.2 us: band_term(): h = jnp.dot(columns, bands[query], preferred_element_type=jnp.float32)]
    psum x1 -> x0, blocking collectives: 29.9 us -> none  [local(): summed = lax.psum(terms, 'seq')]
    unnamed x15 -> x1, local copies, waits for them, and re-layouts: 18.4 us -> 1.24 us
    concatenate x1 -> x0, other arithmetic: 10.7 us -> none  [local(): far_pack = jnp.concatenate([columns_of(2), out_grads, member_wire], axis=1)]
    slice x2 -> x0, local copies, waits for them, and re-layouts: 6.86 us -> none  [local(): got_grads = got[:, band_rows:band_rows + width]]
    ppermute x2 -> x0, starting transfers between devices: 6.01 us -> none  [shifted(): return lax.ppermute(x, axis, [(i, (i + by) % peers) for i in range(peers)])]
  transfers between devices with their start and end apart: 2 -> 0, of which waited for: 2 -> 0; matrix products, arithmetic and copies ran while one was open for 12% -> 0% of each run, Pallas kernels for 0% -> 0%
where the time goes in v1:
time: 101 us
  Pallas kernels  99.8 us (99%)
  local copies, waits for them, and re-layouts  1.24 us (1%)
    pallas_call x1, Pallas kernels, local(): pl.pallas_call(functools.partial(kernel, count, chunk), out_shape=jax.Sha...  99.8 us

profile of v1, /device:TPU:0, one launch (start us, length us, event | category | flops | bytes accessed | tf_op | source)
XLA Modules:
  0.0 101.0 jit_solution(7839114294614335259)
XLA Ops:
  0.0 99.8 %shard_map.55 = f32[2,2]{1,0:T(2,128)} custom-call(bf16[128,8192]{1,0:T(8,128)(2,1)} %act_ref.1, bf16[128,14336]{1,0:T(8,128)(2,1)} %grad_ref.1, bf16[2,512,14336]{2,1,0:T(8,128)(2,1)} %query_ref.1, s32[1,128]{1,0:T(1,128)} %seg_ref.1, s32[1,4]{1,0:T(1,128)} %seq_ref.1), custom_call_target="tpu_custom_call" | custom-call | flops 11274289152 | bytes 29360128 | tf_op jit(solution)/shard_map/pallas_call | solution.py:253
  99.8 1.2 %copy.7 = f32[2,2]{1,0:T(2,128)} copy(f32[2,2]{1,0:T(2,128)} %shard_map.55) | data formatting | bytes 32

commit v2 on v1

--- a/solution.py
+++ b/solution.py
@@ -26,12 +26,15 @@
     held_grad,
     held_act,
     held_sid,
+    held_seg,
+    held_seq,
     acc,
     term_mine,
     term_got,
     query_sem,
     own_sem,
     act_sem,
+    id_sem,
     far_send,
     far_recv,
     near_send,
@@ -127,21 +130,17 @@
         )
 
     barrier = pltpu.get_barrier_semaphore()
-
-    @pl.loop(1, count)
-    def _(d):
+    for d in range(1, count):
         pl.semaphore_signal(
             barrier,
             inc=1,
             device_id=(group, lax.rem(me + d, count)),
             device_id_type=MESH,
         )
-
-    sid = jnp.zeros((1, tokens), jnp.int32)
-    for s in range(SEGS):
-        sid = sid + jnp.where(seg_ref[...] == s, seq_ref[0, s], 0)
-    held_sid[0] = jnp.broadcast_to(sid.astype(jnp.float32), held_sid.shape[1:])
-    acc[...] = jnp.zeros_like(acc)
+    seg_copy = pltpu.make_async_copy(seg_ref, held_seg, id_sem.at[0])
+    seq_copy = pltpu.make_async_copy(seq_ref, held_seq, id_sem.at[1])
+    seg_copy.start()
+    seq_copy.start()
     pl.semaphore_wait(barrier, count - 1)
 
     @pl.loop(0, chunks)
@@ -154,15 +153,23 @@
         def _(k):
             near_copy(k).start()
 
-    for copy in side_copies():
-        copy.start()
-    own_act = pltpu.make_async_copy(columns(me), held_act.at[0], act_sem)
-    own_act.start()
-
     @pl.loop(0, chunks)
     def _(k):
         query_copy(k).start()
         own_copy(k).start()
+
+    own_act = pltpu.make_async_copy(columns(me), held_act.at[0], act_sem)
+    own_act.start()
+    seg_copy.wait()
+    seq_copy.wait()
+    sid = jnp.zeros((1, tokens), jnp.int32)
+    for s in range(SEGS):
+        sid = sid + jnp.where(held_seg[...] == s, held_seq[0, s], 0)
+    held_sid[0] = jnp.broadcast_to(sid.astype(jnp.float32), held_sid.shape[1:])
+    sides = side_copies()
+    for copy in sides:
+        copy.start()
+    acc[...] = jnp.zeros_like(acc)
 
     def add(k, slot):
         for q in range(queries):
@@ -188,26 +195,27 @@
         near_copy(k).wait_recv()
         add(k, 1)
 
-    own_act.wait()
-    for copy in side_copies():
-        copy.wait_recv()
+    sides[1].wait_recv()
+    sides[3].wait_recv()
     lanes = lax.broadcasted_iota(jnp.int32, (tokens, pad), 1).astype(jnp.float32)
-    rows = [jnp.zeros((1, pad), jnp.float32) for _ in range(queries)]
+    members = []
     for slot in range(3):
         ids = jnp.broadcast_to(held_sid[slot][0:1, :], (tokens, tokens)).T
-        member = (lanes == ids[:, 0:1]).astype(jnp.float32)
+        members.append((lanes == ids[:, 0:1]).astype(jnp.float32))
+    rows = [jnp.zeros((1, pad), jnp.float32) for _ in range(queries)]
+    for slot, ready in ((0, own_act.wait), (1, sides[0].wait_recv), (2, sides[2].wait_recv)):
+        ready()
         act = held_act[slot].astype(jnp.float32)
         for q in range(queries):
             value = jnp.sum(acc[slot, q] * act, axis=1, keepdims=True)
-            rows[q] = rows[q] + jnp.sum(value * member, axis=0, keepdims=True)
+            rows[q] = rows[q] + jnp.sum(value * members[slot], axis=0, keepdims=True)
     sub = lax.broadcasted_iota(jnp.int32, term_mine.shape, 0)
     mine = jnp.zeros(term_mine.shape, jnp.float32)
     for q in range(queries):
         mine = jnp.where(sub == q, jnp.broadcast_to(rows[q], term_mine.shape), mine)
     term_mine[...] = mine
 
-    @pl.loop(1, count)
-    def _(d):
+    for d in range(1, count):
         term_copy(d).start()
 
     @pl.loop(0, chunks)
@@ -215,7 +223,7 @@
         far_copy(k).wait_send()
         near_copy(k).wait_send()
 
-    for copy in side_copies():
+    for copy in sides:
         copy.wait_send()
 
     def gather(d, total):
@@ -257,8 +265,8 @@
             whole,
             whole,
             whole,
-            pl.BlockSpec(memory_space=pltpu.VMEM),
-            pl.BlockSpec(memory_space=pltpu.SMEM),
+            whole,
+            whole,
         ],
         out_specs=pl.BlockSpec(memory_space=pltpu.VMEM),
         scratch_shapes=[
@@ -266,12 +274,15 @@
             pltpu.VMEM((3, chunks, tokens, chunk), jnp.bfloat16),
             pltpu.VMEM((3, tokens, band), jnp.bfloat16),
             pltpu.VMEM((3, 8, tokens), jnp.float32),
+            pltpu.VMEM(segment_ids.shape, jnp.int32),
+            pltpu.SMEM(sequence_ids.shape, jnp.int32),
             pltpu.VMEM((3, queries, tokens, band), jnp.float32),
             pltpu.VMEM((sub, pad), jnp.float32),
             pltpu.VMEM((count, sub, pad), jnp.float32),
             dma((chunks,)),
             dma((chunks,)),
             dma,
+            dma((2,)),
             dma((chunks,)),
             dma((chunks,)),
             dma((chunks,)),

time: 101 us -> 101 us (level)
  no operation moved by 1% of the time
where the time goes in v2:
time: 101 us; the launch traced here: 100 us
  Pallas kernels  99.2 us (98%)
  local copies, waits for them, and re-layouts  1.24 us (1%)
    pallas_call x1, Pallas kernels, local(): pl.pallas_call(functools.partial(kernel, count, chunk), out_shape=jax.Sha...  99.2 us

profile of v2, /device:TPU:0, one launch (start us, length us, event | category | flops | bytes accessed | tf_op | source)
XLA Modules:
  0.0 100.4 jit_solution(9779083563480526761)
XLA Ops:
  0.0 99.2 %shard_map.55 = f32[2,2]{1,0:T(2,128)} custom-call(bf16[128,8192]{1,0:T(8,128)(2,1)} %act_ref.1, bf16[128,14336]{1,0:T(8,128)(2,1)} %grad_ref.1, bf16[2,512,14336]{2,1,0:T(8,128)(2,1)} %query_ref.1, s32[1,128]{1,0:T(1,128)} %seg_ref.1, s32[1,4]{1,0:T(1,128)} %seq_ref.1), custom_call_target="tpu_custom_call" | custom-call | flops 11274289152 | bytes 29360128 | tf_op jit(solution)/shard_map/pallas_call | solution.py:261
  99.2 1.2 %copy.7 = f32[2,2]{1,0:T(2,128)} copy(f32[2,2]{1,0:T(2,128)} %shard_map.55) | data formatting | bytes 32

commit v3 on v2

--- a/solution.py
+++ b/solution.py
@@ -167,7 +167,7 @@
         sid = sid + jnp.where(held_seg[...] == s, held_seq[0, s], 0)
     held_sid[0] = jnp.broadcast_to(sid.astype(jnp.float32), held_sid.shape[1:])
     sides = side_copies()
-    for copy in sides:
+    for copy in sides[1::2] + sides[0::2]:
         copy.start()
     acc[...] = jnp.zeros_like(acc)
 

time: 101 us -> 100 us (0.990)
  no operation moved by 1% of the time
where the time goes in v3:
time: 100 us
  Pallas kernels  98.7 us (99%)
  local copies, waits for them, and re-layouts  1.24 us (1%)
    pallas_call x1, Pallas kernels, local(): pl.pallas_call(functools.partial(kernel, count, chunk), out_shape=jax.Sha...  98.7 us

profile of v3, /device:TPU:0, one launch (start us, length us, event | category | flops | bytes accessed | tf_op | source)
XLA Modules:
  0.0 100.0 jit_solution(2603048922907528617)
XLA Ops:
  0.0 98.7 %shard_map.55 = f32[2,2]{1,0:T(2,128)} custom-call(bf16[128,8192]{1,0:T(8,128)(2,1)} %act_ref.1, bf16[128,14336]{1,0:T(8,128)(2,1)} %grad_ref.1, bf16[2,512,14336]{2,1,0:T(8,128)(2,1)} %query_ref.1, s32[1,128]{1,0:T(1,128)} %seg_ref.1, s32[1,4]{1,0:T(1,128)} %seq_ref.1), custom_call_target="tpu_custom_call" | custom-call | flops 11274289152 | bytes 29360128 | tf_op jit(solution)/shard_map/pallas_call | solution.py:261
  98.7 1.2 %copy.7 = f32[2,2]{1,0:T(2,128)} copy(f32[2,2]{1,0:T(2,128)} %shard_map.55) | data formatting | bytes 32
